TPU v7x, 32 devices: a whole 2x2x4 slice. The times are simulated.
32 devices in a mesh: prow: 4 (over x, core), pcol: 8 (over z, y).
Axes of the slice: x: 2, y: 2, z: 4, core: 2. Of those that a mesh axis runs over, the one named last changes fastest.
Arguments:
- velocity_u: bfloat16 [128, 1024, 1024], P('prow', 'pcol'), may hold values from -6 to 6
- velocity_v: bfloat16 [128, 1024, 1024], P('prow', 'pcol'), may hold values from -6 to 6
- velocity_w: bfloat16 [128, 1024, 1024], P('prow', 'pcol'), may hold values from -6 to 6
- x_derivative: bfloat16 [1024, 1024], P('pcol'), may hold values from -2 to 2
- y_derivative: bfloat16 [128, 128], replicated, may hold values from -2 to 2
- z_derivative: bfloat16 [1024, 1024], P('prow'), may hold values from -2 to 2
Outputs:
- u_tendency: float32 [128, 1024, 1024], P('pcol', 'prow')
- divergence: float32 [1024, 1024, 128], P('pcol', 'prow')
All inputs are finite; a program needn't handle non-finite values.
Results may differ from a plain program's by a relative error of at most 0.0018.
Values may be sent and summed in bfloat16 or wider, within the bound.
A program may use at most 256 MiB of HBM per device.

v0:
```python
import jax
import jax.numpy as jnp
from jax import lax
from jax.sharding import PartitionSpec as P


def body(velocity_u, velocity_v, velocity_w, x_derivative, y_derivative, z_derivative):
    y_rows, z_cols, x_full = velocity_u.shape
    flat_u = velocity_u.reshape(y_rows * z_cols, x_full)
    u_dx = lax.dot_general(
        flat_u,
        lax.all_gather(x_derivative, "pcol", axis=0, tiled=True),
        (((1,), (1,)), ((), ())),
        preferred_element_type=jnp.float32,
    )
    u_dx = u_dx.reshape(y_rows, z_cols, x_full).astype(jnp.bfloat16)
    u_ypen, v_ypen, w_ypen, dx_ypen = (
        lax.all_to_all(velocity_u, "prow", split_axis=2, concat_axis=0, tiled=True),
        lax.all_to_all(velocity_v, "prow", split_axis=2, concat_axis=0, tiled=True),
        lax.all_to_all(velocity_w, "prow", split_axis=2, concat_axis=0, tiled=True),
        lax.all_to_all(u_dx, "prow", split_axis=2, concat_axis=0, tiled=True),
    )
    y_full, z_local, x_local = u_ypen.shape
    u_dy = jnp.dot(
        y_derivative, u_ypen.reshape(y_full, z_local * x_local), preferred_element_type=jnp.float32
    ).reshape(y_full, z_local, x_local)
    v_dy = jnp.dot(
        y_derivative, v_ypen.reshape(y_full, z_local * x_local), preferred_element_type=jnp.float32
    ).reshape(y_full, z_local, x_local)
    dx_float = dx_ypen.astype(jnp.float32)
    partial_div = dx_float + v_dy
    advect = u_ypen.astype(jnp.float32) * dx_float + v_ypen.astype(jnp.float32) * u_dy
    u_turned = jnp.transpose(u_ypen, (0, 2, 1))
    w_turned = jnp.transpose(w_ypen, (0, 2, 1))
    u_zpen, w_zpen = (
        lax.all_to_all(u_turned, "pcol", split_axis=0, concat_axis=2, tiled=True),
        lax.all_to_all(w_turned, "pcol", split_axis=0, concat_axis=2, tiled=True),
    )
    stacked = jnp.stack([u_zpen, w_zpen])
    slopes = jnp.einsum(
        "ak,syxk->syxa",
        lax.all_gather(z_derivative, "prow", axis=0, tiled=True),
        stacked,
        preferred_element_type=jnp.float32,
    )
    u_dz = slopes[0]
    w_dz = slopes[1]
    part_turned = jnp.transpose(partial_div, (0, 2, 1))
    adv_turned = jnp.transpose(advect, (0, 2, 1))
    part_zpen, adv_zpen = (
        lax.all_to_all(part_turned, "pcol", split_axis=0, concat_axis=2, tiled=True),
        lax.all_to_all(adv_turned, "pcol", split_axis=0, concat_axis=2, tiled=True),
    )
    u_tendency = -(adv_zpen + w_zpen.astype(jnp.float32) * u_dz)
    div_zpen = jnp.transpose(part_zpen + w_dz, (2, 1, 0))
    divergence = lax.all_to_all(div_zpen, "pcol", split_axis=0, concat_axis=2, tiled=True)
    return (u_tendency, divergence)


def solution(mesh):
    in_specs = (
        P("prow", "pcol", None),
        P("prow", "pcol", None),
        P("prow", "pcol", None),
        P("pcol", None),
        P(),
        P("prow", None),
    )
    out_specs = (P("pcol", "prow", None), P("pcol", "prow", None))
    return jax.shard_map(body, mesh=mesh, in_specs=in_specs, out_specs=out_specs, check_vma=False)
```

profile of v0, /device:TPU:0, one launch (start us, length us, event | category | flops | bytes accessed | tf_op | source)
XLA Modules:
  0.0 2019.2 jit_solution(14387424407352621265)
XLA Ops:
  38.7 81.3 %all-to-all-done = bf16[32,128,1024]{1,0,2:T(8,128)(2,1)} async-done(((bf16[32,128,1024]{1,0,2:T(8,128)(2,1)}), bf16[32,128,1024]{1,0,2:T(8,128)(2,1)}, u32[]{:S(2)}, u32[]{:S(2)}) %all-to-all-start) | async-done | bytes 8388640 | tf_op jit(solution)/shard_map/all_to_all | solution.py:18
  138.2 80.7 %all-to-all-done.2 = bf16[32,128,1024]{1,0,2:T(8,128)(2,1)} async-done(((bf16[32,128,1024]{1,0,2:T(8,128)(2,1)}), bf16[32,128,1024]{1,0,2:T(8,128)(2,1)}, u32[]{:S(2)}, u32[]{:S(2)}) %all-to-all-start.2) | async-done | bytes 8388640 | tf_op jit(solution)/shard_map/all_to_all | solution.py:19
  225.2 54.1 %all-gather.3.cloned.1.call-done = bf16[1024,1024]{1,0:T(8,128)(2,1)} async-done(((bf16[128,1024]{1,0:T(8,128)(2,1)}), bf16[1024,1024]{1,0:T(8,128)(2,1)}) %all-gather.3.cloned.1.call-update) | async-done | bytes 2097168 | tf_op jit(solution)/shard_map/all_gather | solution.py:12
  279.3 14.9 convolution_convert_fusion
  323.5 15.9 copy.74
  351.0 65.7 %all-to-all-done.1 = bf16[32,128,1024]{1,0,2:T(8,128)(2,1)} async-done(((bf16[32,128,1024]{1,0,2:T(8,128)(2,1)}), bf16[32,128,1024]{1,0,2:T(8,128)(2,1)}, u32[]{:S(2)}, u32[]{:S(2)}) %all-to-all-start.1) | async-done | bytes 8388640 | tf_op jit(solution)/shard_map/all_to_all | solution.py:21
  423.3 13.7 copy.85
  437.1 169.2 %all-to-all-done.6 = bf16[128,256,128]{1,2,0:T(8,128)(2,1)} async-done(((bf16[128,256,128]{1,2,0:T(8,128)(2,1)}), bf16[128,256,128]{1,2,0:T(8,128)(2,1)}, u32[]{:S(2)}, u32[]{:S(2)}) %all-to-all-start.6) | async-done | bytes 8388640 | tf_op jit(solution)/shard_map/all_to_all | solution.py:36
  611.8 13.8 copy.78
  637.4 17.8 copy.79
  655.2 13.7 copy.73
  693.2 17.0 copy.76
  710.2 24.8 %fusion.9 = f32[128,256,128]{1,0,2:T(8,128)} fusion(bf16[128,256,128]{2,1,0:T(8,128)(2,1)} %bitcast.124, f32[4,32,128,256]{3,1,0,2:T(8,128)} %copy.79, f32[32,128,4,256]{3,0,2,1:T(8,128)} %copy.76, bf16[128,128,256]{2,0,1:T(8,128)(2,1)} %bitcast.112, bf16[128,128]{1,0:T(8,128)(2,1)S(1)} %copy-done), kind=kOutput, calls=%fused_computation.16 | convolution fusion | flops 1090519040 | bytes 67141632 | tf_op jit(solution)/shard_map/dot_general | solution.py:24
  735.0 17.7 copy.81
  752.7 41.0 %all-to-all-done.5 = bf16[128,256,128]{1,2,0:T(8,128)(2,1)} async-done(((bf16[128,256,128]{1,2,0:T(8,128)(2,1)}), bf16[128,256,128]{1,2,0:T(8,128)(2,1)}, u32[]{:S(2)}, u32[]{:S(2)}) %all-to-all-start.5) | async-done | bytes 8388640 | tf_op jit(solution)/shard_map/all_to_all | solution.py:37
  823.9 16.7 fusion.10
  840.6 17.8 copy.92
  858.4 302.2 %all-to-all-done.3 = f32[128,256,128]{1,2,0:T(8,128)} async-done(((f32[128,256,128]{1,2,0:T(8,128)}), f32[128,256,128]{1,2,0:T(8,128)}, u32[]{:S(2)}, u32[]{:S(2)}) %all-to-all-start.3) | async-done | bytes 16777248 | tf_op jit(solution)/shard_map/all_to_all | solution.py:52
  1166.9 13.0 copy.89
  1179.9 13.4 stack.9
  1193.3 12.8 copy.90
  1206.1 13.3 stack.10
  1231.3 26.2 %fusion.4 = f32[2,16,256,1024]{3,2,1,0:T(8,128)} fusion(bf16[1,16,256,1024]{3,2,1,0:T(8,128)(2,1)} %stack.10, bf16[1,16,256,1024]{3,2,1,0:T(8,128)(2,1)} %stack.9, bf16[1024,1024]{1,0:T(8,128)(2,1)} %all-gather.5.cloned.1.call-done), kind=kOutput, calls=%fused_computation.7 | convolution fusion | flops 17188257792 | bytes 52428800 | tf_op jit(solution)/shard_map/ak,syxk->syxa/dot_general | solution.py:40
  1257.5 17.8 copy.82
  1275.3 18.0 all_to_all.116
  1293.3 235.0 %all-to-all-done.7 = f32[128,256,128]{1,2,0:T(8,128)} async-done(((f32[128,256,128]{1,2,0:T(8,128)}), f32[128,256,128]{1,2,0:T(8,128)}, u32[]{:S(2)}, u32[]{:S(2)}) %all-to-all-start.7) | async-done | bytes 16777248 | tf_op jit(solution)/shard_map/all_to_all | solution.py:51
  1528.4 17.8 copy.93
  1546.2 18.0 all_to_all.130
  1564.2 37.8 %fusion.3 = (f32[1024,256,16]{0,1,2:T(8,128)}, f32[16,256,1024]{2,1,0:T(8,128)}) fusion(f32[16,256,1024]{2,1,0:T(8,128)} %all_to_all.130, f32[2,16,256,1024]{3,2,1,0:T(8,128)} %fusion.4, f32[16,256,1024]{2,1,0:T(8,128)} %all_to_all.116, bf16[16,256,8,128]{3,1,0,2:T(8,128)(2,1)} %bitcast.123), kind=kLoop, calls=%fused_computation.5 | loop fusion | flops 20971520 | bytes 109051904 | tf_op jit(solution)/shard_map/transpose | solution.py:55
  1601.9 17.5 copy.94
  1619.5 367.6 %all_to_all.144 = f32[1024,256,16]{1,2,0:T(8,128)S(1)} all-to-all(f32[1024,256,16]{1,2,0:T(8,128)} %copy.94), channel_id=1, replica_groups=mesh['prow'=4,'pcol'=8] {'pcol'}, dimensions={0} | all-to-all | bytes 33554432 | tf_op jit(solution)/shard_map/all_to_all | solution.py:56
  1994.0 17.4 copy.96
  (30 shorter events, 199.7 us)
Async XLA Ops:
  8.0 702.2 %copy-start = (bf16[128,128]{1,0:T(8,128)(2,1)S(1)}, bf16[128,128]{1,0:T(8,128)(2,1)}, u32[]{:S(2)}) copy-start(bf16[128,128]{1,0:T(8,128)(2,1)} %param.10) | copy-start | bytes 98308
  20.5 99.5 %all-to-all-start = ((bf16[32,128,1024]{1,0,2:T(8,128)(2,1)}), bf16[32,128,1024]{1,0,2:T(8,128)(2,1)}, u32[]{:S(2)}, u32[]{:S(2)}) async-start(bf16[32,128,1024]{1,0,2:T(8,128)(2,1)} %copy.72), calls=%async_computation | async-start | bytes 16777216 | tf_op jit(solution)/shard_map/all_to_all | solution.py:18
  120.0 98.9 %all-to-all-start.2 = ((bf16[32,128,1024]{1,0,2:T(8,128)(2,1)}), bf16[32,128,1024]{1,0,2:T(8,128)(2,1)}, u32[]{:S(2)}, u32[]{:S(2)}) async-start(bf16[32,128,1024]{1,0,2:T(8,128)(2,1)} %copy.77), calls=%async_computation.2 | async-start | bytes 16777216 | tf_op jit(solution)/shard_map/all_to_all | solution.py:19
  218.8 98.8 %all-to-all-start.4 = ((bf16[32,128,1024]{1,0,2:T(8,128)(2,1)}), bf16[32,128,1024]{1,0,2:T(8,128)(2,1)}, u32[]{:S(2)}, u32[]{:S(2)}) async-start(bf16[32,128,1024]{1,0,2:T(8,128)(2,1)} %copy.83), calls=%async_computation.4 | async-start | bytes 16777216 | tf_op jit(solution)/shard_map/all_to_all | solution.py:20
  224.5 54.8 %all-gather.3.cloned.1.call-start = ((), (), s32[]{:S(2)}) async-start(), calls=%async_computation.9 | async-start | bytes 2359296 | tf_op jit(solution)/shard_map/all_gather | solution.py:12
  317.6 99.1 %all-to-all-start.1 = ((bf16[32,128,1024]{1,0,2:T(8,128)(2,1)}), bf16[32,128,1024]{1,0,2:T(8,128)(2,1)}, u32[]{:S(2)}, u32[]{:S(2)}) async-start(bf16[32,128,1024]{1,0,2:T(8,128)(2,1)} %copy.75), calls=%async_computation.1 | async-start | bytes 16777216 | tf_op jit(solution)/shard_map/all_to_all | solution.py:21
  416.7 189.6 %all-to-all-start.6 = ((bf16[128,256,128]{1,2,0:T(8,128)(2,1)}), bf16[128,256,128]{1,2,0:T(8,128)(2,1)}, u32[]{:S(2)}, u32[]{:S(2)}) async-start(bf16[128,256,128]{1,2,0:T(8,128)(2,1)} %copy.88), calls=%async_computation.6 | async-start | bytes 16777216 | tf_op jit(solution)/shard_map/all_to_all | solution.py:36
  606.3 187.4 %all-to-all-start.5 = ((bf16[128,256,128]{1,2,0:T(8,128)(2,1)}), bf16[128,256,128]{1,2,0:T(8,128)(2,1)}, u32[]{:S(2)}, u32[]{:S(2)}) async-start(bf16[128,256,128]{1,2,0:T(8,128)(2,1)} %bitcast.117), calls=%async_computation.5 | async-start | bytes 16777216 | tf_op jit(solution)/shard_map/all_to_all | solution.py:37
  793.7 366.9 %all-to-all-start.3 = ((f32[128,256,128]{1,2,0:T(8,128)}), f32[128,256,128]{1,2,0:T(8,128)}, u32[]{:S(2)}, u32[]{:S(2)}) async-start(f32[128,256,128]{1,2,0:T(8,128)} %copy.81), calls=%async_computation.3 | async-start | bytes 33554432 | tf_op jit(solution)/shard_map/all_to_all | solution.py:52
  1160.6 367.7 %all-to-all-start.7 = ((f32[128,256,128]{1,2,0:T(8,128)}), f32[128,256,128]{1,2,0:T(8,128)}, u32[]{:S(2)}, u32[]{:S(2)}) async-start(f32[128,256,128]{1,2,0:T(8,128)} %copy.92), calls=%async_computation.7 | async-start | bytes 33554432 | tf_op jit(solution)/shard_map/all_to_all | solution.py:51
  1166.3 65.0 %all-gather.5.cloned.1.call-start = ((), (), s32[]{:S(2)}) async-start(), calls=%async_computation.10 | async-start | bytes 2621440 | tf_op jit(solution)/shard_map/all_gather | solution.py:42
  1994.0 17.4 copy-start.1
Sparse Core Ops, SparseCore 0:
  227.4 51.7 all-gather.2
Sparse Core Ops, SparseCore 1:
  1168.4 23.0 all-gather.4
where the time goes:
time: 2030 us; the launch traced here: 2020 us
  waiting for transfers between devices  1040 us (51%)
  local copies, waits for them, and re-layouts  416 us (20%)
  blocking collectives  368 us (18%)
  matrix products  82.6 us (4%)
  other arithmetic  49.7 us (2%)
  starting transfers between devices  46.4 us (2%)
    all_to_all x1, blocking collectives, body(): lax.all_to_all(div_zpen, 'pcol', split_axis=0, concat_axis=2, tiled=True)  368 us
    all_to_all x1, waiting for transfers between devices, body(): lax.all_to_all(adv_turned, 'pcol', split_axis=0, concat_axis=2, tiled=True)  302 us
    all_to_all x1, waiting for transfers between devices, body(): lax.all_to_all(part_turned, 'pcol', split_axis=0, concat_axis=2, tiled=True)  235 us
    all_to_all x1, waiting for transfers between devices, body(): lax.all_to_all(u_turned, 'pcol', split_axis=0, concat_axis=2, tiled=True)  169 us
    all_to_all x1, waiting for transfers between devices, body(): lax.all_to_all(velocity_u, 'prow', split_axis=2, concat_axis=0, tiled=True)  81.3 us
    all_to_all x1, waiting for transfers between devices, body(): lax.all_to_all(velocity_v, 'prow', split_axis=2, concat_axis=0, tiled=True)  80.7 us
    unnamed x10, local copies, waits for them, and re-layouts  79.8 us
    all_to_all x1, waiting for transfers between devices, body(): lax.all_to_all(u_dx, 'prow', split_axis=2, concat_axis=0, tiled=True)  65.7 us
  transfers between devices with their start and end apart: 10, of which 9 were waited for; matrix products, arithmetic and copies ran while one was open for 20% of the time, Pallas kernels for 0%

commit v1 on v0

v1 whole, which is shorter than its diff:
```python
import functools
import jax
import jax.numpy as jnp
from jax import lax
from jax.experimental import pallas as pl
from jax.experimental.pallas import tpu as pltpu
from jax.sharding import PartitionSpec as P

F32 = jnp.float32
BF16 = jnp.bfloat16
MIB = 1 << 20


def turn_kernel(rows, *refs):
    count = (len(refs) - 3) // 2
    srcs, dsts = refs[:count], refs[count:2 * count]
    send_sem, recv_sem, own_sem = refs[2 * count:]
    me = lax.axis_index("prow")
    barrier = pltpu.get_barrier_semaphore()
    for k in range(1, rows):
        pl.semaphore_signal(
            barrier, inc=1, device_id={"prow": lax.rem(me + k, rows)}, device_id_type=pl.DeviceIdType.MESH
        )
    pl.semaphore_wait(barrier, rows - 1)

    copies = []
    for n, (src, dst) in enumerate(zip(srcs, dsts)):
        width = dst.shape[-1]

        def columns(q):
            return src.at[:, :, pl.ds(pl.multiple_of(q * width, width), width)]

        for k in range(1, rows):
            q = lax.rem(me + k, rows)
            copy = pltpu.make_async_remote_copy(
                src_ref=columns(q),
                dst_ref=dst.at[me],
                send_sem=send_sem.at[n, k],
                recv_sem=recv_sem.at[n, k],
                device_id={"prow": q},
                device_id_type=pl.DeviceIdType.MESH,
            )
            copy.start()
            copies.append(copy)
        own = pltpu.make_async_copy(columns(me), dst.at[me], own_sem.at[n])
        own.start()
        copies.append(own)
    for copy in copies:
        copy.wait()


def turn(arrays, rows, number):
    y, z, x = arrays[0].shape
    width = x // rows
    if width % 128:
        sent = [a.reshape(y, z, rows, width).transpose(2, 0, 1, 3) for a in arrays]
        return [lax.all_to_all(a, "prow", 0, 0, tiled=True).reshape(rows * y, z, width) for a in sent]
    count = len(arrays)
    outs = pl.pallas_call(
        functools.partial(turn_kernel, rows),
        out_shape=[jax.ShapeDtypeStruct((rows, y, z, width), a.dtype) for a in arrays],
        in_specs=[pl.BlockSpec(memory_space=pl.ANY)] * count,
        out_specs=[pl.BlockSpec(memory_space=pl.ANY)] * count,
        scratch_shapes=[
            pltpu.SemaphoreType.DMA((count, rows)),
            pltpu.SemaphoreType.DMA((count, rows)),
            pltpu.SemaphoreType.DMA((count,)),
        ],
        compiler_params=pltpu.CompilerParams(collective_id=number, has_side_effects=True),
        cost_estimate=pl.CostEstimate(flops=0, bytes_accessed=250 * MIB * count, transcendentals=0),
        name=f"turn_{number}",
    )(*arrays)
    return [out.reshape(rows * y, z, width) for out in outs]


def exchange(array):
    return lax.all_to_all(array, "pcol", 0, 0, tiled=True)


def advect_kernel(u_ref, v_ref, dx_ref, yd_ref, out_ref):
    yd = yd_ref[...]
    for i in range(u_ref.shape[0]):
        u = u_ref[i]
        u_dy = jnp.dot(yd, u, preferred_element_type=F32)
        adv = u.astype(F32) * dx_ref[i].astype(F32) + v_ref[i].astype(F32) * u_dy
        out_ref[i] = adv.astype(out_ref.dtype)


def advection(u, v, dx, yd):
    z, y, x = u.shape
    zb = min(8, z)
    spec = pl.BlockSpec((zb, y, x), lambda i: (i, 0, 0))
    return pl.pallas_call(
        advect_kernel,
        grid=(z // zb,),
        out_shape=jax.ShapeDtypeStruct((z, y, x), BF16),
        in_specs=[spec, spec, spec, pl.BlockSpec((y, y), lambda i: (0, 0))],
        out_specs=spec,
        compiler_params=pltpu.CompilerParams(vmem_limit_bytes=32 * MIB),
        cost_estimate=pl.CostEstimate(flops=2 * z * y * y * x, bytes_accessed=8 * z * y * x, transcendentals=0),
        name="advection",
    )(u, v, dx, yd)


def div_kernel(v_ref, dx_ref, wdz_ref, yd_ref, out_ref):
    yd = yd_ref[...]
    for i in range(v_ref.shape[0]):
        v_dy = jnp.dot(yd, v_ref[i], preferred_element_type=F32)
        w_dz = wdz_ref[:, i].astype(F32).reshape(v_dy.shape)
        total = (dx_ref[i].astype(F32) + v_dy) + w_dz
        out_ref[i] = total.T


def divergence_of(v, dx, wdz, yd):
    z, y, x = v.shape
    parts, _, yl, _ = wdz.shape
    zb = min(8, z)
    spec = pl.BlockSpec((zb, y, x), lambda i: (i, 0, 0))
    wdz_spec = pl.BlockSpec((parts, zb, yl, x), lambda i: (0, i, 0, 0))
    return pl.pallas_call(
        div_kernel,
        grid=(z // zb,),
        out_shape=jax.ShapeDtypeStruct((z, x, y), F32),
        in_specs=[spec, spec, wdz_spec, pl.BlockSpec((y, y), lambda i: (0, 0))],
        out_specs=pl.BlockSpec((zb, x, y), lambda i: (i, 0, 0)),
        compiler_params=pltpu.CompilerParams(vmem_limit_bytes=32 * MIB),
        cost_estimate=pl.CostEstimate(flops=2 * z * y * y * x, bytes_accessed=10 * z * y * x, transcendentals=0),
        name="divergence",
    )(v, dx, wdz, yd)


def slope_kernel(w_ref, zd_ref, out_ref):
    parts, _, z, x = w_ref.shape
    w = w_ref[...].reshape(parts * z, x)
    slope = jnp.dot(zd_ref[...], w, preferred_element_type=F32)
    out_ref[...] = slope.astype(out_ref.dtype).reshape(out_ref.shape)


def z_slope(w, zd):
    parts, y, z, x = w.shape
    spec = pl.BlockSpec((parts, 1, z, x), lambda i: (0, i, 0, 0))
    full = parts * z
    return pl.pallas_call(
        slope_kernel,
        grid=(y,),
        out_shape=jax.ShapeDtypeStruct(w.shape, BF16),
        in_specs=[spec, pl.BlockSpec((full, full), lambda i: (0, 0))],
        out_specs=spec,
        compiler_params=pltpu.CompilerParams(vmem_limit_bytes=40 * MIB),
        cost_estimate=pl.CostEstimate(flops=2 * y * full * full * x, bytes_accessed=4 * y * full * x, transcendentals=0),
        name="z_slope",
    )(w, zd)


def tendency_kernel(u_ref, w_ref, adv_ref, zd_ref, out_ref):
    parts, _, z, x = w_ref.shape
    u = u_ref[...].reshape(parts * z, x)
    for c in range(parts):
        slope = jnp.dot(zd_ref[c * z:(c + 1) * z, :], u, preferred_element_type=F32)
        total = -(adv_ref[c, 0].astype(F32) + w_ref[c, 0].astype(F32) * slope)
        out_ref[0, :, c * z:(c + 1) * z] = total.T


def tendency(u, w, adv, zd):
    parts, y, z, x = w.shape
    spec = pl.BlockSpec((parts, 1, z, x), lambda i: (0, i, 0, 0))
    full = parts * z
    return pl.pallas_call(
        tendency_kernel,
        grid=(y,),
        out_shape=jax.ShapeDtypeStruct((y, x, full), F32),
        in_specs=[spec, spec, spec, pl.BlockSpec((full, full), lambda i: (0, 0))],
        out_specs=pl.BlockSpec((1, x, full), lambda i: (i, 0, 0)),
        compiler_params=pltpu.CompilerParams(vmem_limit_bytes=40 * MIB),
        cost_estimate=pl.CostEstimate(flops=2 * y * full * full * x, bytes_accessed=10 * y * full * x, transcendentals=0),
        name="tendency",
    )(u, w, adv, zd)


def after(array, *earlier):
    return lax.optimization_barrier((array, *earlier))[0]


def body(rows, cols, u, v, w, x_derivative, yd, z_derivative):
    y, z, x = u.shape
    xl, yl = x // rows, rows * y // cols
    y_full = rows * y
    plain = xl % 128 != 0 or z % 128 != 0

    (w_y,) = turn([w], rows, 0)
    xd = lax.all_gather(x_derivative, "pcol", axis=0, tiled=True)
    zd = lax.all_gather(z_derivative, "prow", axis=0, tiled=True)
    w_z = exchange(w_y.reshape(cols, yl, z, xl))

    u_y, v_y = turn([after(u, w_y), v], rows, 1)
    u_dx = lax.dot_general(
        u.reshape(y * z, x), xd, (((1,), (1,)), ((), ())), preferred_element_type=F32
    ).astype(BF16).reshape(y, z, x)
    (dx_y,) = turn([after(u_dx, v_y)], rows, 2)

    u_z = exchange(after(u_y, w_z).reshape(cols, yl, z, xl))
    u_t, v_t, dx_t = (jnp.transpose(a, (1, 0, 2)) for a in (u_y, v_y, dx_y))
    if plain:
        w_dz = jnp.einsum(
            "ak,kyx->ayx", zd, jnp.transpose(w_z, (0, 2, 1, 3)).reshape(cols * z, yl, xl), preferred_element_type=F32
        )
        w_dz = w_dz.astype(BF16).reshape(cols, z, yl, xl)
        u_dy = jnp.einsum("ab,zbx->zax", yd, u_t, preferred_element_type=F32)
        adv_t = (u_t.astype(F32) * dx_t.astype(F32) + v_t.astype(F32) * u_dy).astype(BF16)
    else:
        w_dz = jnp.transpose(z_slope(w_z, zd), (0, 2, 1, 3))
        adv_t = advection(u_t, v_t, dx_t, yd)
    wdz_y = exchange(after(w_dz, u_z))
    adv_y = jnp.transpose(adv_t, (1, 0, 2)).reshape(cols, yl, z, xl)
    adv_z = exchange(after(adv_y, wdz_y))
    if plain:
        wdz_t = jnp.transpose(wdz_y, (1, 0, 2, 3)).reshape(z, y_full, xl)
        v_dy = jnp.einsum("ab,zbx->zax", yd, v_t, preferred_element_type=F32)
        divergence = jnp.transpose(dx_t.astype(F32) + v_dy + wdz_t.astype(F32), (0, 2, 1))
        u_line, w_line, adv_line = (
            jnp.transpose(a, (1, 3, 0, 2)).reshape(yl, xl, cols * z) for a in (u_z, w_z, adv_z)
        )
        u_dz = jnp.einsum("ak,yxk->yxa", zd, u_line, preferred_element_type=F32)
        u_tendency = -(adv_line.astype(F32) + w_line.astype(F32) * u_dz)
    else:
        divergence = divergence_of(v_t, dx_t, wdz_y, yd)
        u_tendency = tendency(u_z, w_z, adv_z, zd)
    return u_tendency, divergence


def solution(mesh):
    in_specs = (
        P("prow", "pcol", None),
        P("prow", "pcol", None),
        P("prow", "pcol", None),
        P("pcol", None),
        P(),
        P("prow", None),
    )
    out_specs = (P("pcol", "prow", None), P("pcol", "prow", None))
    step = functools.partial(body, mesh.shape["prow"], mesh.shape["pcol"])
    return jax.shard_map(step, mesh=mesh, in_specs=in_specs, out_specs=out_specs, check_vma=False)
```

time: 2030 us -> 1060 us (0.52)
  waiting for transfers between devices: 1040 us -> 475 us
  Pallas kernels: 0 us -> 437 us
  blocking collectives: 368 us -> 0 us
  local copies, waits for them, and re-layouts: 416 us -> 87.6 us
  matrix products: 82.6 us -> 15.2 us
  other arithmetic: 49.7 us -> 0 us
  starting transfers between devices: 46.4 us -> 21.8 us
    all_to_all x8 -> x4, waiting for transfers between devices: 986 us -> 287 us  [exchange(): return lax.all_to_all(array, 'pcol', 0, 0, tiled=True)]
    pallas_call x0 -> x7, Pallas kernels: none -> 437 us  [the longest x3 368 us: turn(): pl.pallas_call(functools.partial(turn_kernel, rows), out_shape=[jax.Shape...]
    all_to_all x1 -> x0, blocking collectives: 368 us -> none  [body(): lax.all_to_all(div_zpen, 'pcol', split_axis=0, concat_axis=2, tiled=True)]
    all_to_all x12 -> x0, local copies, waits for them, and re-layouts: 173 us -> none  [the longest x2 35.8 us: body(): lax.all_to_all(adv_turned, 'pcol', split_axis=0, concat_axis=2, tiled=True)]
    all_gather x2, waiting for transfers between devices: 54.1 us -> 187 us  [the longest x1 162 us: body(): xd = lax.all_gather(x_derivative, 'pcol', axis=0, tiled=True)]
    dot_general x4 -> x1, matrix products: 82.6 us -> 15.2 us  [body(): lax.dot_general(u.reshape(y * z, x), xd, (((1,), (1,)), ((), ())), prefer...]
    unnamed x10 -> x16, local copies, waits for them, and re-layouts: 79.8 us -> 18.4 us
    transpose x4 -> x1, local copies, waits for them, and re-layouts: 64.6 us -> 11.4 us  [body(): adv_y = jnp.transpose(adv_t, (1, 0, 2)).reshape(cols, yl, z, xl)]
  transfers between devices with their start and end apart: 10 -> 6, of which waited for: 9 -> 4; matrix products, arithmetic and copies ran while one was open for 20% -> 7% of each run, Pallas kernels for 0% -> 30%
where the time goes in v1:
time: 1060 us; the launch traced here: 1050 us
  waiting for transfers between devices  475 us (45%)
  Pallas kernels  437 us (41%)
  local copies, waits for them, and re-layouts  87.6 us (8%)
  starting transfers between devices  21.8 us (2%)
  between operations  16 us (2%)
  matrix products  15.2 us (1%)
    pallas_call x3, Pallas kernels, turn(): pl.pallas_call(functools.partial(turn_kernel, rows), out_shape=[jax.Shape...  368 us
    all_to_all x4, waiting for transfers between devices, exchange(): return lax.all_to_all(array, 'pcol', 0, 0, tiled=True)  287 us
    all_gather x1, waiting for transfers between devices, body(): xd = lax.all_gather(x_derivative, 'pcol', axis=0, tiled=True)  162 us
    pallas_call x3, local copies, waits for them, and re-layouts, turn(): pl.pallas_call(functools.partial(turn_kernel, rows), out_shape=[jax.Shape...  34.5 us
    all_gather x1, waiting for transfers between devices, body(): zd = lax.all_gather(z_derivative, 'prow', axis=0, tiled=True)  25.6 us
    pallas_call x1, Pallas kernels, tendency(): pl.pallas_call(tendency_kernel, grid=(y,), out_shape=jax.ShapeDtypeStruct...  22.9 us
    all_to_all x4, starting transfers between devices, exchange(): return lax.all_to_all(array, 'pcol', 0, 0, tiled=True)  21.6 us
  transfers between devices with their start and end apart: 6, of which 4 were waited for; matrix products, arithmetic and copies ran while one was open for 7% of the time, Pallas kernels for 30%

profile of v1, /device:TPU:0, one launch (start us, length us, event | category | flops | bytes accessed | tf_op | source)
XLA Modules:
  0.0 1052.8 jit_solution(15680676152943900423)
XLA Ops:
  8.0 93.8 %turn_0.1 = bf16[4,32,128,256]{3,2,1,0:T(8,128)(2,1)} custom-call(bf16[32,128,1024]{2,1,0:T(8,128)(2,1)} %refs_0_.2), custom_call_target="tpu_custom_call" | custom-call | bytes 262144000 | tf_op jit(solution)/shard_map/turn_0/pallas_call | solution.py:59
  101.8 5.8 all-to-all-start
  107.7 182.4 %turn_1.1 = (bf16[4,32,128,256]{3,2,1,0:T(8,128)(2,1)}, bf16[4,32,128,256]{3,2,1,0:T(8,128)(2,1)}) custom-call(bf16[32,128,1024]{2,1,0:T(8,128)(2,1)} %refs_0_.1, bf16[32,128,1024]{2,1,0:T(8,128)(2,1)} %refs_1_.1), custom_call_target="tpu_custom_call" | custom-call | bytes 524288000 | tf_op jit(solution)/shard_map/turn_1/pallas_call | solution.py:59
  290.1 11.5 %copy.8 = bf16[4,32,128,256]{3,1,0,2:T(8,128)(2,1)} copy(bf16[4,32,128,256]{3,2,1,0:T(8,128)(2,1)} %get-tuple-element.8) | data formatting | bytes 16777216 | tf_op jit(solution)/shard_map/turn_1/pallas_call | solution.py:59
  301.6 11.5 %copy.9 = bf16[128,128,256]{2,1,0:T(8,128)(2,1)} copy(bf16[128,128,256]{2,0,1:T(8,128)(2,1)} %bitcast.20) | data formatting | bytes 16777216 | tf_op jit(solution)/shard_map/optimization_barrier | solution.py:181
  313.2 5.7 all-to-all-start.1
  318.9 0.2 all-gather.5.cloned.1.call-start
  319.1 0.5 all-gather.5.cloned.1.call-update
  319.6 25.6 %all-gather.5.cloned.1.call-done.zd_ref = bf16[1024,1024]{1,0:T(8,128)(2,1)} async-done(((bf16[256,1024]{1,0:T(8,128)(2,1)}), bf16[1024,1024]{1,0:T(8,128)(2,1)}) %all-gather.5.cloned.1.call-update) | async-done | bytes 2097168 | tf_op jit(solution)/shard_map/all_gather | solution.py:192
  345.2 1.6 copy-done.5
  346.8 15.3 %z_slope.1 = bf16[8,16,128,256]{3,2,1,0:T(8,128)(2,1)S(1)} custom-call(bf16[8,16,128,256]{3,2,1,0:T(8,128)(2,1)} %all-to-all-done.w_ref, bf16[1024,1024]{1,0:T(8,128)(2,1)S(1)} %copy-done.5), custom_call_target="tpu_custom_call" | custom-call | flops 8589934592 | bytes 16777216 | tf_op jit(solution)/shard_map/z_slope/pallas_call | solution.py:143
  362.1 3.2 copy-done.4
  365.3 11.8 %copy.15 = bf16[8,16,128,256]{3,1,2,0:T(8,128)(2,1)} copy(bf16[8,16,128,256]{3,2,1,0:T(8,128)(2,1)} %copy-done.4) | data formatting | bytes 16777216 | tf_op jit(solution)/shard_map/z_slope/pallas_call | solution.py:143
  377.1 126.1 %all-to-all-done.1.u_ref = bf16[8,16,128,256]{3,2,1,0:T(8,128)(2,1)} async-done(((bf16[8,16,128,256]{3,2,1,0:T(8,128)(2,1)}), bf16[8,16,128,256]{3,2,1,0:T(8,128)(2,1)}, u32[]{:S(2)}, u32[]{:S(2)}) %all-to-all-start.1) | async-done | bytes 8388640 | tf_op jit(solution)/shard_map/all_to_all | solution.py:77
  503.2 5.0 all-to-all-start.2
  508.2 0.0 all-gather.3.cloned.1.call-start
  508.2 0.5 all-gather.3.cloned.1.call-update
  508.7 11.5 %copy.10 = bf16[4,32,128,256]{3,1,0,2:T(8,128)(2,1)} copy(bf16[4,32,128,256]{3,2,1,0:T(8,128)(2,1)} %get-tuple-element.10) | data formatting | bytes 16777216 | tf_op jit(solution)/shard_map/turn_1/pallas_call | solution.py:59
  520.3 161.5 %all-gather.3.cloned.1.call-done = bf16[1024,1024]{1,0:T(8,128)(2,1)} async-done(((bf16[128,1024]{1,0:T(8,128)(2,1)}), bf16[1024,1024]{1,0:T(8,128)(2,1)}) %all-gather.3.cloned.1.call-update) | async-done | bytes 2097168 | tf_op jit(solution)/shard_map/all_gather | solution.py:191
  681.8 15.2 %convolution_convert_fusion = bf16[4096,1024]{1,0:T(8,128)(2,1)} fusion(bf16[4096,1024]{1,0:T(8,128)(2,1)} %bitcast.31, bf16[1024,1024]{1,0:T(8,128)(2,1)} %all-gather.3.cloned.1.call-done), kind=kOutput, calls=%fused_computation.1 | convolution fusion | flops 8594128896 | bytes 18874368 | tf_op jit(solution)/shard_map/dot_general | solution.py:196
  697.0 92.2 %turn_2.1 = bf16[4,32,128,256]{3,2,1,0:T(8,128)(2,1)} custom-call(bf16[32,128,1024]{2,1,0:T(8,128)(2,1)} %bitcast.32), custom_call_target="tpu_custom_call" | custom-call | bytes 262144000 | tf_op jit(solution)/shard_map/turn_2/pallas_call | solution.py:59
  789.3 11.4 %copy.11 = bf16[4,32,128,256]{3,1,0,2:T(8,128)(2,1)} copy(bf16[4,32,128,256]{3,2,1,0:T(8,128)(2,1)} %turn_2.1) | data formatting | bytes 16777216 | tf_op jit(solution)/shard_map/turn_2/pallas_call | solution.py:59
  800.6 3.4 copy-done
  804.0 13.4 %advection.1 = bf16[128,128,256]{2,1,0:T(8,128)(2,1)S(1)} custom-call(bf16[128,128,256]{2,1,0:T(8,128)(2,1)S(1)} %bitcast.21, bf16[128,128,256]{2,1,0:T(8,128)(2,1)} %bitcast.22, bf16[128,128,256]{2,1,0:T(8,128)(2,1)} %bitcast.24, bf16[128,128]{1,0:T(8,128)(2,1)S(1)} %copy-done.7), custom_call_target="tpu_custom_call" | custom-call | flops 1073741824 | bytes 33554432 | tf_op jit(solution)/shard_map/advection/pallas_call | solution.py:93
  817.5 3.4 copy-done.3
  820.8 11.4 %copy.12 = bf16[128,128,256]{2,1,0:T(8,128)(2,1)} copy(bf16[128,128,256]{2,0,1:T(8,128)(2,1)} %bitcast.26) | data formatting | bytes 16777216 | tf_op jit(solution)/shard_map/transpose | solution.py:214
  832.2 5.0 all-to-all-start.3
  837.3 3.4 copy-done.1
  840.6 3.4 copy-done.2
  844.0 16.9 %divergence.1 = f32[128,256,128]{2,1,0:T(8,128)} custom-call(bf16[128,128,256]{2,1,0:T(8,128)(2,1)S(1)} %bitcast.23, bf16[128,128,256]{2,1,0:T(8,128)(2,1)S(1)} %bitcast.25, bf16[8,128,16,256]{3,2,1,0:T(8,128)(2,1)} %all-to-all-done.2.wdz_ref, bf16[128,128]{1,0:T(8,128)(2,1)S(1)} %copy-done.7), custom_call_target="tpu_custom_call" | custom-call | flops 1073741824 | bytes 41943040 | tf_op jit(solution)/shard_map/divergence/pallas_call | solution.py:120
  860.9 161.1 %all-to-all-done.3.adv_ref = bf16[8,16,128,256]{3,2,1,0:T(8,128)(2,1)} async-done(((bf16[8,16,128,256]{3,2,1,0:T(8,128)(2,1)}), bf16[8,16,128,256]{3,2,1,0:T(8,128)(2,1)}, u32[]{:S(2)}, u32[]{:S(2)}) %all-to-all-start.3) | async-done | bytes 8388640 | tf_op jit(solution)/shard_map/all_to_all | solution.py:77
  1022.0 22.9 %tendency.1 = f32[16,256,1024]{2,1,0:T(8,128)} custom-call(bf16[8,16,128,256]{3,2,1,0:T(8,128)(2,1)} %all-to-all-done.1.u_ref, bf16[8,16,128,256]{3,2,1,0:T(8,128)(2,1)} %all-to-all-done.w_ref, bf16[8,16,128,256]{3,2,1,0:T(8,128)(2,1)} %all-to-all-done.3.adv_ref, bf16[1024,1024]{1,0:T(8,128)(2,1)S(1)} %copy-done.6), custom_call_target="tpu_custom_call" | custom-call | flops 8589934592 | bytes 41943040 | tf_op jit(solution)/shard_map/tendency/pallas_call | solution.py:168
  (12 shorter events, 0.0 us)
Async XLA Ops:
  101.8 199.8 %all-to-all-start = ((bf16[8,16,128,256]{3,2,1,0:T(8,128)(2,1)}), bf16[8,16,128,256]{3,2,1,0:T(8,128)(2,1)}, u32[]{:S(2)}, u32[]{:S(2)}) async-start(bf16[8,16,128,256]{3,2,1,0:T(8,128)(2,1)} %bitcast.30), calls=%async_computation | async-start | bytes 16777216 | tf_op jit(solution)/shard_map/all_to_all | solution.py:77
  313.2 190.0 %all-to-all-start.1 = ((bf16[8,16,128,256]{3,2,1,0:T(8,128)(2,1)}), bf16[8,16,128,256]{3,2,1,0:T(8,128)(2,1)}, u32[]{:S(2)}, u32[]{:S(2)}) async-start(bf16[8,16,128,256]{3,2,1,0:T(8,128)(2,1)} %bitcast.28), calls=%async_computation.1 | async-start | bytes 16777216 | tf_op jit(solution)/shard_map/all_to_all | solution.py:77
  318.9 26.3 %all-gather.5.cloned.1.call-start = ((), (), s32[]{:S(2)}) async-start(), calls=%async_computation.5 | async-start | bytes 2621440 | tf_op jit(solution)/shard_map/all_gather | solution.py:192
  345.2 1.6 copy-start.5
  362.1 3.3 copy-start.4
  503.2 329.0 %all-to-all-start.2 = ((bf16[8,128,16,256]{3,2,1,0:T(8,128)(2,1)}), bf16[8,128,16,256]{3,2,1,0:T(8,128)(2,1)}, u32[]{:S(2)}, u32[]{:S(2)}) async-start(bf16[8,128,16,256]{3,2,1,0:T(8,128)(2,1)} %bitcast.27), calls=%async_computation.2 | async-start | bytes 16777216 | tf_op jit(solution)/shard_map/all_to_all | solution.py:77
  508.2 173.7 %all-gather.3.cloned.1.call-start = ((), (), s32[]{:S(2)}) async-start(), calls=%async_computation.4 | async-start | bytes 2359296 | tf_op jit(solution)/shard_map/all_gather | solution.py:191
  789.2 11.4 %copy-start.7 = (bf16[128,128]{1,0:T(8,128)(2,1)S(1)}, bf16[128,128]{1,0:T(8,128)(2,1)}, u32[]{:S(2)}) copy-start(bf16[128,128]{1,0:T(8,128)(2,1)} %yd_ref.3) | copy-start | bytes 98308
  800.6 3.4 copy-start
  817.4 3.4 copy-start.3
  832.2 189.8 %all-to-all-start.3 = ((bf16[8,16,128,256]{3,2,1,0:T(8,128)(2,1)}), bf16[8,16,128,256]{3,2,1,0:T(8,128)(2,1)}, u32[]{:S(2)}, u32[]{:S(2)}) async-start(bf16[8,16,128,256]{3,2,1,0:T(8,128)(2,1)} %bitcast.29), calls=%async_computation.3 | async-start | bytes 16777216 | tf_op jit(solution)/shard_map/all_to_all | solution.py:77
  837.3 3.4 copy-start.1
  840.6 3.4 copy-start.2
  844.0 178.0 %copy-start.6 = (bf16[1024,1024]{1,0:T(8,128)(2,1)S(1)}, bf16[1024,1024]{1,0:T(8,128)(2,1)}, u32[]{:S(2)}) copy-start(bf16[1024,1024]{1,0:T(8,128)(2,1)} %all-gather.5.cloned.1.call-done.zd_ref) | copy-start | bytes 6291460
Sparse Core Ops, SparseCore 0:
  321.3 23.8 all-gather.4
Sparse Core Ops, SparseCore 1:
  510.8 171.0 all-gather.2

commit v2 on v1

--- a/solution.py
+++ b/solution.py
@@ -11,10 +11,10 @@
 MIB = 1 << 20
 
 
-def turn_kernel(rows, *refs):
-    count = (len(refs) - 3) // 2
-    srcs, dsts = refs[:count], refs[count:2 * count]
-    send_sem, recv_sem, own_sem = refs[2 * count:]
+def turn_kernel(rows, ready, *refs):
+    count = (len(refs) - 3 - ready) // 2
+    srcs, dsts = refs[:count], refs[count + ready:2 * count + ready]
+    send_sem, recv_sem, own_sem = refs[2 * count + ready:]
     me = lax.axis_index("prow")
     barrier = pltpu.get_barrier_semaphore()
     for k in range(1, rows):
@@ -49,7 +49,7 @@
         copy.wait()
 
 
-def turn(arrays, rows, number):
+def turn(arrays, rows, number, ready=()):
     y, z, x = arrays[0].shape
     width = x // rows
     if width % 128:
@@ -57,9 +57,9 @@
         return [lax.all_to_all(a, "prow", 0, 0, tiled=True).reshape(rows * y, z, width) for a in sent]
     count = len(arrays)
     outs = pl.pallas_call(
-        functools.partial(turn_kernel, rows),
+        functools.partial(turn_kernel, rows, len(ready)),
         out_shape=[jax.ShapeDtypeStruct((rows, y, z, width), a.dtype) for a in arrays],
-        in_specs=[pl.BlockSpec(memory_space=pl.ANY)] * count,
+        in_specs=[pl.BlockSpec(memory_space=pl.ANY)] * (count + len(ready)),
         out_specs=[pl.BlockSpec(memory_space=pl.ANY)] * count,
         scratch_shapes=[
             pltpu.SemaphoreType.DMA((count, rows)),
@@ -69,7 +69,7 @@
         compiler_params=pltpu.CompilerParams(collective_id=number, has_side_effects=True),
         cost_estimate=pl.CostEstimate(flops=0, bytes_accessed=250 * MIB * count, transcendentals=0),
         name=f"turn_{number}",
-    )(*arrays)
+    )(*arrays, *ready)
     return [out.reshape(rows * y, z, width) for out in outs]
 
 
@@ -129,14 +129,14 @@
     )(v, dx, wdz, yd)
 
 
-def slope_kernel(w_ref, zd_ref, out_ref):
+def slope_kernel(w_ref, zd_ref, _, out_ref):
     parts, _, z, x = w_ref.shape
     w = w_ref[...].reshape(parts * z, x)
     slope = jnp.dot(zd_ref[...], w, preferred_element_type=F32)
     out_ref[...] = slope.astype(out_ref.dtype).reshape(out_ref.shape)
 
 
-def z_slope(w, zd):
+def z_slope(w, zd, ready):
     parts, y, z, x = w.shape
     spec = pl.BlockSpec((parts, 1, z, x), lambda i: (0, i, 0, 0))
     full = parts * z
@@ -144,12 +144,12 @@
         slope_kernel,
         grid=(y,),
         out_shape=jax.ShapeDtypeStruct(w.shape, BF16),
-        in_specs=[spec, pl.BlockSpec((full, full), lambda i: (0, 0))],
+        in_specs=[spec, pl.BlockSpec((full, full), lambda i: (0, 0)), pl.BlockSpec(memory_space=pl.ANY)],
         out_specs=spec,
         compiler_params=pltpu.CompilerParams(vmem_limit_bytes=40 * MIB),
         cost_estimate=pl.CostEstimate(flops=2 * y * full * full * x, bytes_accessed=4 * y * full * x, transcendentals=0),
         name="z_slope",
-    )(w, zd)
+    )(w, zd, ready)
 
 
 def tendency_kernel(u_ref, w_ref, adv_ref, zd_ref, out_ref):
@@ -187,8 +187,8 @@
     y_full = rows * y
     plain = xl % 128 != 0 or z % 128 != 0
 
-    (w_y,) = turn([w], rows, 0)
     xd = lax.all_gather(x_derivative, "pcol", axis=0, tiled=True)
+    (w_y,) = turn([w], rows, 0, [xd])
     zd = lax.all_gather(z_derivative, "prow", axis=0, tiled=True)
     w_z = exchange(w_y.reshape(cols, yl, z, xl))
 
@@ -208,7 +208,7 @@
         u_dy = jnp.einsum("ab,zbx->zax", yd, u_t, preferred_element_type=F32)
         adv_t = (u_t.astype(F32) * dx_t.astype(F32) + v_t.astype(F32) * u_dy).astype(BF16)
     else:
-        w_dz = jnp.transpose(z_slope(w_z, zd), (0, 2, 1, 3))
+        w_dz = jnp.transpose(z_slope(w_z, zd, v_y), (0, 2, 1, 3))
         adv_t = advection(u_t, v_t, dx_t, yd)
     wdz_y = exchange(after(w_dz, u_z))
     adv_y = jnp.transpose(adv_t, (1, 0, 2)).reshape(cols, yl, z, xl)

time: 1060 us -> 972 us (0.917)
  waiting for transfers between devices: 475 us -> 388 us
    all_gather x1, waiting for transfers between devices: 162 us -> 54.2 us  [body(): xd = lax.all_gather(x_derivative, 'pcol', axis=0, tiled=True)]
    all_to_all x4, waiting for transfers between devices: 287 us -> 307 us  [exchange(): return lax.all_to_all(array, 'pcol', 0, 0, tiled=True)]
  transfers between devices with their start and end apart: 6 -> 6, of which waited for: 4 -> 5; matrix products, arithmetic and copies ran while one was open for 7% -> 8% of each run, Pallas kernels for 30% -> 33%
where the time goes in v2:
time: 972 us; the launch traced here: 963 us
  Pallas kernels  435 us (45%)
  waiting for transfers between devices  388 us (40%)
  local copies, waits for them, and re-layouts  87.7 us (9%)
  starting transfers between devices  21 us (2%)
  between operations  16 us (2%)
  matrix products  14.9 us (2%)
    pallas_call x3, Pallas kernels, turn(): pl.pallas_call(functools.partial(turn_kernel, rows, len(ready)), out_shap...  367 us
    all_to_all x4, waiting for transfers between devices, exchange(): return lax.all_to_all(array, 'pcol', 0, 0, tiled=True)  307 us
    all_gather x1, waiting for transfers between devices, body(): xd = lax.all_gather(x_derivative, 'pcol', axis=0, tiled=True)  54.2 us
    pallas_call x3, local copies, waits for them, and re-layouts, turn(): pl.pallas_call(functools.partial(turn_kernel, rows, len(ready)), out_shap...  34.6 us
    all_gather x1, waiting for transfers between devices, body(): zd = lax.all_gather(z_derivative, 'prow', axis=0, tiled=True)  25.2 us
    pallas_call x1, Pallas kernels, tendency(): pl.pallas_call(tendency_kernel, grid=(y,), out_shape=jax.ShapeDtypeStruct...  22.9 us
    all_to_all x4, starting transfers between devices, exchange(): return lax.all_to_all(array, 'pcol', 0, 0, tiled=True)  20.8 us
  transfers between devices with their start and end apart: 6, of which 5 were waited for; matrix products, arithmetic and copies ran while one was open for 8% of the time, Pallas kernels for 33%

profile of v2, /device:TPU:0, one launch (start us, length us, event | category | flops | bytes accessed | tf_op | source)
XLA Modules:
  0.0 962.6 jit_solution(5735157883840059751)
XLA Ops:
  8.0 0.7 all-gather.3.cloned.1.call-update
  8.7 54.2 %all-gather.3.cloned.1.call-done.refs_1_ = bf16[1024,1024]{1,0:T(8,128)(2,1)} async-done(((bf16[128,1024]{1,0:T(8,128)(2,1)}), bf16[1024,1024]{1,0:T(8,128)(2,1)}) %all-gather.3.cloned.1.call-update) | async-done | bytes 2097168 | tf_op jit(solution)/shard_map/all_gather | solution.py:190
  63.0 92.3 %turn_0.1 = bf16[4,32,128,256]{3,2,1,0:T(8,128)(2,1)} custom-call(bf16[32,128,1024]{2,1,0:T(8,128)(2,1)} %refs_0_.2, bf16[1024,1024]{1,0:T(8,128)(2,1)} %all-gather.3.cloned.1.call-done.refs_1_), custom_call_target="tpu_custom_call" | custom-call | bytes 262144000 | tf_op jit(solution)/shard_map/turn_0/pallas_call | solution.py:59
  155.3 5.0 all-to-all-start
  160.3 182.7 %turn_1.1 = (bf16[4,32,128,256]{3,2,1,0:T(8,128)(2,1)}, bf16[4,32,128,256]{3,2,1,0:T(8,128)(2,1)}) custom-call(bf16[32,128,1024]{2,1,0:T(8,128)(2,1)} %refs_0_.1, bf16[32,128,1024]{2,1,0:T(8,128)(2,1)} %refs_1_.1), custom_call_target="tpu_custom_call" | custom-call | bytes 524288000 | tf_op jit(solution)/shard_map/turn_1/pallas_call | solution.py:59
  343.0 11.5 %copy.8 = bf16[4,32,128,256]{3,1,0,2:T(8,128)(2,1)} copy(bf16[4,32,128,256]{3,2,1,0:T(8,128)(2,1)} %get-tuple-element.8) | data formatting | bytes 16777216 | tf_op jit(solution)/shard_map/turn_1/pallas_call | solution.py:59
  354.6 11.5 %copy.9 = bf16[128,128,256]{2,1,0:T(8,128)(2,1)} copy(bf16[128,128,256]{2,0,1:T(8,128)(2,1)} %bitcast.21) | data formatting | bytes 16777216 | tf_op jit(solution)/shard_map/optimization_barrier | solution.py:181
  366.1 5.6 all-to-all-start.1
  371.7 0.2 all-gather.5.cloned.1.call-start
  371.9 0.3 all-gather.5.cloned.1.call-update
  372.3 25.2 %all-gather.5.cloned.1.call-done.zd_ref = bf16[1024,1024]{1,0:T(8,128)(2,1)} async-done(((bf16[256,1024]{1,0:T(8,128)(2,1)}), bf16[1024,1024]{1,0:T(8,128)(2,1)}) %all-gather.5.cloned.1.call-update) | async-done | bytes 2097168 | tf_op jit(solution)/shard_map/all_gather | solution.py:192
  397.4 1.6 copy-done.5
  399.0 15.3 %z_slope.1 = bf16[8,16,128,256]{3,2,1,0:T(8,128)(2,1)S(1)} custom-call(bf16[8,16,128,256]{3,2,1,0:T(8,128)(2,1)} %all-to-all-done.w_ref, bf16[1024,1024]{1,0:T(8,128)(2,1)S(1)} %copy-done.5, bf16[128,128,256]{2,1,0:T(8,128)(2,1)} %bitcast.33), custom_call_target="tpu_custom_call" | custom-call | flops 8589934592 | bytes 16777216 | tf_op jit(solution)/shard_map/z_slope/pallas_call | solution.py:143
  414.3 3.2 copy-done.4
  417.5 11.8 %copy.17 = bf16[8,16,128,256]{3,1,2,0:T(8,128)(2,1)} copy(bf16[8,16,128,256]{3,2,1,0:T(8,128)(2,1)} %copy-done.4) | data formatting | bytes 16777216 | tf_op jit(solution)/shard_map/z_slope/pallas_call | solution.py:143
  429.3 126.5 %all-to-all-done.1.u_ref = bf16[8,16,128,256]{3,2,1,0:T(8,128)(2,1)} async-done(((bf16[8,16,128,256]{3,2,1,0:T(8,128)(2,1)}), bf16[8,16,128,256]{3,2,1,0:T(8,128)(2,1)}, u32[]{:S(2)}, u32[]{:S(2)}) %all-to-all-start.1) | async-done | bytes 8388640 | tf_op jit(solution)/shard_map/all_to_all | solution.py:77
  555.9 5.2 all-to-all-start.2
  561.1 11.7 %copy.10 = bf16[4,32,128,256]{3,1,0,2:T(8,128)(2,1)} copy(bf16[4,32,128,256]{3,2,1,0:T(8,128)(2,1)} %get-tuple-element.10) | data formatting | bytes 16777216 | tf_op jit(solution)/shard_map/turn_1/pallas_call | solution.py:59
  572.8 14.9 %convolution_convert_fusion = bf16[4096,1024]{1,0:T(8,128)(2,1)} fusion(bf16[4096,1024]{1,0:T(8,128)(2,1)} %bitcast.32, bf16[1024,1024]{1,0:T(8,128)(2,1)S(1)} %copy-done.8), kind=kOutput, calls=%fused_computation.1 | convolution fusion | flops 8594128896 | bytes 18874368 | tf_op jit(solution)/shard_map/dot_general | solution.py:196
  587.6 91.8 %turn_2.1 = bf16[4,32,128,256]{3,2,1,0:T(8,128)(2,1)} custom-call(bf16[32,128,1024]{2,1,0:T(8,128)(2,1)} %bitcast.34), custom_call_target="tpu_custom_call" | custom-call | bytes 262144000 | tf_op jit(solution)/shard_map/turn_2/pallas_call | solution.py:59
  679.5 11.4 %copy.11 = bf16[4,32,128,256]{3,1,0,2:T(8,128)(2,1)} copy(bf16[4,32,128,256]{3,2,1,0:T(8,128)(2,1)} %turn_2.1) | data formatting | bytes 16777216 | tf_op jit(solution)/shard_map/turn_2/pallas_call | solution.py:59
  690.9 3.4 copy-done
  694.3 13.2 %advection.1 = bf16[128,128,256]{2,1,0:T(8,128)(2,1)S(1)} custom-call(bf16[128,128,256]{2,1,0:T(8,128)(2,1)S(1)} %bitcast.22, bf16[128,128,256]{2,1,0:T(8,128)(2,1)} %bitcast.23, bf16[128,128,256]{2,1,0:T(8,128)(2,1)} %bitcast.25, bf16[128,128]{1,0:T(8,128)(2,1)S(1)} %copy-done.7), custom_call_target="tpu_custom_call" | custom-call | flops 1073741824 | bytes 33554432 | tf_op jit(solution)/shard_map/advection/pallas_call | solution.py:93
  707.4 3.4 copy-done.3
  710.8 11.4 %copy.12 = bf16[128,128,256]{2,1,0:T(8,128)(2,1)} copy(bf16[128,128,256]{2,0,1:T(8,128)(2,1)} %bitcast.27) | data formatting | bytes 16777216 | tf_op jit(solution)/shard_map/transpose | solution.py:214
  722.2 22.1 %all-to-all-done.2.wdz_ref = bf16[8,128,16,256]{3,2,1,0:T(8,128)(2,1)} async-done(((bf16[8,128,16,256]{3,2,1,0:T(8,128)(2,1)}), bf16[8,128,16,256]{3,2,1,0:T(8,128)(2,1)}, u32[]{:S(2)}, u32[]{:S(2)}) %all-to-all-start.2) | async-done | bytes 8388640 | tf_op jit(solution)/shard_map/all_to_all | solution.py:77
  744.3 5.0 all-to-all-start.3
  749.4 3.4 copy-done.1
  752.7 3.4 copy-done.2
  756.1 16.9 %divergence.1 = f32[128,256,128]{2,1,0:T(8,128)} custom-call(bf16[128,128,256]{2,1,0:T(8,128)(2,1)S(1)} %bitcast.24, bf16[128,128,256]{2,1,0:T(8,128)(2,1)S(1)} %bitcast.26, bf16[8,128,16,256]{3,2,1,0:T(8,128)(2,1)} %all-to-all-done.2.wdz_ref, bf16[128,128]{1,0:T(8,128)(2,1)S(1)} %copy-done.7), custom_call_target="tpu_custom_call" | custom-call | flops 1073741824 | bytes 41943040 | tf_op jit(solution)/shard_map/divergence/pallas_call | solution.py:120
  773.0 158.8 %all-to-all-done.3.adv_ref = bf16[8,16,128,256]{3,2,1,0:T(8,128)(2,1)} async-done(((bf16[8,16,128,256]{3,2,1,0:T(8,128)(2,1)}), bf16[8,16,128,256]{3,2,1,0:T(8,128)(2,1)}, u32[]{:S(2)}, u32[]{:S(2)}) %all-to-all-start.3) | async-done | bytes 8388640 | tf_op jit(solution)/shard_map/all_to_all | solution.py:77
  931.8 22.9 %tendency.1 = f32[16,256,1024]{2,1,0:T(8,128)} custom-call(bf16[8,16,128,256]{3,2,1,0:T(8,128)(2,1)} %all-to-all-done.1.u_ref, bf16[8,16,128,256]{3,2,1,0:T(8,128)(2,1)} %all-to-all-done.w_ref, bf16[8,16,128,256]{3,2,1,0:T(8,128)(2,1)} %all-to-all-done.3.adv_ref, bf16[1024,1024]{1,0:T(8,128)(2,1)S(1)} %copy-done.6), custom_call_target="tpu_custom_call" | custom-call | flops 8589934592 | bytes 41943040 | tf_op jit(solution)/shard_map/tendency/pallas_call | solution.py:168
  (14 shorter events, 0.1 us)
Async XLA Ops:
  8.0 55.0 %all-gather.3.cloned.1.call-start = ((), (), s32[]{:S(2)}) async-start(), calls=%async_computation.4 | async-start | bytes 2359296 | tf_op jit(solution)/shard_map/all_gather | solution.py:190
  155.3 199.3 %all-to-all-start = ((bf16[8,16,128,256]{3,2,1,0:T(8,128)(2,1)}), bf16[8,16,128,256]{3,2,1,0:T(8,128)(2,1)}, u32[]{:S(2)}, u32[]{:S(2)}) async-start(bf16[8,16,128,256]{3,2,1,0:T(8,128)(2,1)} %bitcast.31), calls=%async_computation | async-start | bytes 16777216 | tf_op jit(solution)/shard_map/all_to_all | solution.py:77
  366.1 189.8 %all-to-all-start.1 = ((bf16[8,16,128,256]{3,2,1,0:T(8,128)(2,1)}), bf16[8,16,128,256]{3,2,1,0:T(8,128)(2,1)}, u32[]{:S(2)}, u32[]{:S(2)}) async-start(bf16[8,16,128,256]{3,2,1,0:T(8,128)(2,1)} %bitcast.29), calls=%async_computation.1 | async-start | bytes 16777216 | tf_op jit(solution)/shard_map/all_to_all | solution.py:77
  371.7 25.7 %all-gather.5.cloned.1.call-start = ((), (), s32[]{:S(2)}) async-start(), calls=%async_computation.5 | async-start | bytes 2621440 | tf_op jit(solution)/shard_map/all_gather | solution.py:192
  397.4 1.6 copy-start.5
  414.3 3.3 copy-start.4
  555.9 188.5 %all-to-all-start.2 = ((bf16[8,128,16,256]{3,2,1,0:T(8,128)(2,1)}), bf16[8,128,16,256]{3,2,1,0:T(8,128)(2,1)}, u32[]{:S(2)}, u32[]{:S(2)}) async-start(bf16[8,128,16,256]{3,2,1,0:T(8,128)(2,1)} %bitcast.28), calls=%async_computation.2 | async-start | bytes 16777216 | tf_op jit(solution)/shard_map/all_to_all | solution.py:77
  561.1 11.7 %copy-start.8 = (bf16[1024,1024]{1,0:T(8,128)(2,1)S(1)}, bf16[1024,1024]{1,0:T(8,128)(2,1)}, u32[]{:S(2)}) copy-start(bf16[1024,1024]{1,0:T(8,128)(2,1)} %all-gather.3.cloned.1.call-done.refs_1_) | copy-start | bytes 6291460
  679.5 11.4 %copy-start.7 = (bf16[128,128]{1,0:T(8,128)(2,1)S(1)}, bf16[128,128]{1,0:T(8,128)(2,1)}, u32[]{:S(2)}) copy-start(bf16[128,128]{1,0:T(8,128)(2,1)} %yd_ref.3) | copy-start | bytes 98308
  690.9 3.4 copy-start
  707.4 3.4 copy-start.3
  744.3 187.5 %all-to-all-start.3 = ((bf16[8,16,128,256]{3,2,1,0:T(8,128)(2,1)}), bf16[8,16,128,256]{3,2,1,0:T(8,128)(2,1)}, u32[]{:S(2)}, u32[]{:S(2)}) async-start(bf16[8,16,128,256]{3,2,1,0:T(8,128)(2,1)} %bitcast.30), calls=%async_computation.3 | async-start | bytes 16777216 | tf_op jit(solution)/shard_map/all_to_all | solution.py:77
  749.4 3.4 copy-start.1
  752.7 3.4 copy-start.2
  756.1 175.7 %copy-start.6 = (bf16[1024,1024]{1,0:T(8,128)(2,1)S(1)}, bf16[1024,1024]{1,0:T(8,128)(2,1)}, u32[]{:S(2)}) copy-start(bf16[1024,1024]{1,0:T(8,128)(2,1)} %all-gather.5.cloned.1.call-done.zd_ref) | copy-start | bytes 6291460
Sparse Core Ops, SparseCore 0:
  11.0 51.9 all-gather.2
Sparse Core Ops, SparseCore 1:
  373.7 23.6 all-gather.4
